TPU v7x, 32 devices: a whole 2x2x4 slice. The times are simulated.
32 devices in a mesh: ctx: 4 (over y, x), shard: 4 (over z), replica: 2 (over core).
Axes of the slice: x: 2, y: 2, z: 4, core: 2. Of those that a mesh axis runs over, the one named last changes fastest.
Arguments:
- tokens: bfloat16 [8, 1024, 896], P(('shard', 'replica'), 'ctx'), may hold values from -6 to 6
- block_order: int32 [8, 8], P(('shard', 'replica')), may hold values from 0 to 7, as said below
- w_qkv: bfloat16 [896, 1152], P(('ctx', 'shard')), may hold values from -0.1875 to 0.1875
- qkv_bias: bfloat16 [1152], P(('ctx', 'shard')), may hold values from -3 to 3
- w_out: bfloat16 [896, 896], P(('ctx', 'shard')), may hold values from -1 to 1
- norm_gains: bfloat16 [2, 896], P(None, ('ctx', 'shard')), may hold values from 0.25 to 1.75
- w_gate: bfloat16 [896, 4864], P(('ctx', 'shard')), may hold values from -0.1875 to 0.1875
- w_up: bfloat16 [896, 4864], P(('ctx', 'shard')), may hold values from -0.1875 to 0.1875
- w_down: bfloat16 [4864, 896], P(('ctx', 'shard')), may hold values from -0.078125 to 0.078125
- cotangent: bfloat16 [8, 1024, 896], P(('shard', 'replica'), 'ctx'), may hold values from -6 to 6
Outputs:
- block_out: bfloat16 [8, 1024, 896], P(('shard', 'replica'), 'ctx')
- input_grad: float32 [8, 1024, 896], P(('shard', 'replica'), 'ctx')
- grad_qkv: float32 [896, 1152], P(('ctx', 'shard'))
- grad_bias: float32 [1152], P(('ctx', 'shard'))
- grad_out: float32 [896, 896], P(('ctx', 'shard'))
- grad_gains: float32 [2, 896], P(None, ('ctx', 'shard'))
- grad_gate: float32 [896, 4864], P(('ctx', 'shard'))
- grad_up: float32 [896, 4864], P(('ctx', 'shard'))
- grad_down: float32 [4864, 896], P(('ctx', 'shard'))
Inputs may be any that keep to these rules, and one draw needn't show every extreme that they name: `block_order`: each row lists the 8 block numbers of one sequence, each once, and entries 2 k and 2 k + 1 sum to 7.
All inputs are finite; a program needn't handle non-finite values.
Results may differ from a plain program's by a relative error of at most 0.015.
Values may be sent and summed in bfloat16 or wider, within the bound.
A program may use at most 256 MiB of HBM per device.

v0:
```python
import jax
import jax.numpy as jnp
from jax import lax
from jax.sharding import PartitionSpec as P

Q_HEADS = 14
KV_HEADS = 2
HEAD_DIM = 64
SEQ_LEN = 1024


epsilon = 1e-06
rope_base = 1000000.0
score_scale = 0.125
masked_value = -1e30


def rope_tables(positions):
    half_dim = HEAD_DIM // 2
    inverse = rope_base ** (-(jnp.arange(half_dim, dtype=jnp.float32) * 2.0) / HEAD_DIM)
    angles = positions.astype(jnp.float32)[..., None] * inverse
    angles = jnp.concatenate([angles, angles], axis=-1)
    return (jnp.cos(angles), jnp.sin(angles))


def rotate(values, cosine, sine):
    half_dim = values.shape[-1] // 2
    turned = jnp.concatenate([-values[..., half_dim:], values[..., :half_dim]], axis=-1)
    return values * cosine + turned * sine


def rotate_back(grads, cosine, sine):
    half_dim = grads.shape[-1] // 2
    moved = grads * sine
    turned = jnp.concatenate([moved[..., half_dim:], -moved[..., :half_dim]], axis=-1)
    return grads * cosine + turned


def norm_back(inputs, inverse, gain, upstream):
    scaled = upstream * gain
    gain_term = jnp.sum(upstream * inputs * inverse, axis=0)
    input_term = inverse * scaled - inputs * inverse**3 * jnp.mean(
        scaled * inputs, axis=-1, keepdims=True
    )
    return (gain_term, input_term)


def masked_scores(queries, key_rows, pos_query, pos_key):
    scores = (
        jnp.einsum("qhrd,khd->hrqk", queries, key_rows, preferred_element_type=jnp.float32)
        * score_scale
    )
    allowed = pos_query[:, None] >= pos_key[None, :]
    return jnp.where(allowed, scores, masked_value)


def attend(packed):
    queries, key_rows, value_rows, pos_query, pos_key = packed
    scores = masked_scores(queries, key_rows, pos_query, pos_key)
    top_score = jnp.max(scores, axis=-1, keepdims=True)
    weights = jnp.exp(scores - top_score)
    totals = jnp.sum(weights, axis=-1, keepdims=True)
    attn_probs = (weights / totals).astype(jnp.bfloat16)
    mixed_out = jnp.einsum(
        "hrqk,khd->qhrd", attn_probs, value_rows, preferred_element_type=jnp.float32
    )
    return (mixed_out, top_score + jnp.log(totals))


def attend_back(packed):
    queries, key_rows, value_rows, upstream, logsum, pos_query, pos_key = packed
    scores = masked_scores(queries, key_rows, pos_query, pos_key)
    attn_probs = jnp.exp(scores - logsum)
    dprob = jnp.einsum("qhrd,khd->hrqk", upstream, value_rows, preferred_element_type=jnp.float32)
    row_dot = jnp.sum(attn_probs * dprob, axis=-1, keepdims=True)
    dscore = (attn_probs * (dprob - row_dot)).astype(jnp.bfloat16)
    grad_query = (
        jnp.einsum("hrqk,khd->qhrd", dscore, key_rows, preferred_element_type=jnp.float32)
        * score_scale
    )
    grad_key = (
        jnp.einsum("hrqk,qhrd->khd", dscore, queries, preferred_element_type=jnp.float32)
        * score_scale
    )
    grad_value = jnp.einsum(
        "hrqk,qhrd->khd",
        attn_probs.astype(jnp.bfloat16),
        upstream,
        preferred_element_type=jnp.float32,
    )
    return (grad_query, grad_key, grad_value)


def local(tokens, block_order, w_qkv, qkv_bias, w_out, norm_gains, w_gate, w_up, w_down, cotangent):
    groups, local_len, model_width = tokens.shape
    kv_width = KV_HEADS * HEAD_DIM
    repeats = Q_HEADS // KV_HEADS
    ctx_count = lax.axis_size("ctx")
    ctx_index = lax.axis_index("ctx")
    block_len = local_len // 2
    row_count = groups * local_len
    slots = jnp.arange(SEQ_LEN, dtype=jnp.int32)
    owners = (
        (slots // block_len)[:, None] == jnp.arange(2 * ctx_count, dtype=jnp.int32)[None, :]
    ).astype(jnp.int32)
    positions = (
        jnp.sum(block_order[:, None, :] * owners[None], axis=-1) * block_len + slots % block_len
    )
    own_positions = lax.dynamic_slice_in_dim(positions, ctx_index * local_len, local_len, 1)
    qkv_full, bias_full, out_full, gains_full = (
        lax.all_gather(w_qkv, ("ctx", "shard"), axis=0, tiled=True),
        lax.all_gather(qkv_bias, ("ctx", "shard"), axis=0, tiled=True),
        lax.all_gather(w_out, ("ctx", "shard"), axis=0, tiled=True),
        lax.all_gather(norm_gains, ("ctx", "shard"), axis=1, tiled=True),
    )
    gain_rows = gains_full.astype(jnp.float32)
    resid = tokens.reshape(row_count, model_width).astype(jnp.float32)
    first_inv = lax.rsqrt(jnp.mean(resid * resid, axis=-1, keepdims=True) + epsilon)
    normed_one = (resid * first_inv * gain_rows[0]).astype(jnp.bfloat16)
    projected = jnp.dot(
        normed_one, qkv_full, preferred_element_type=jnp.float32
    ) + bias_full.astype(jnp.float32)
    cosine, sine = rope_tables(own_positions.reshape(row_count))
    query_rows = rotate(
        projected[:, :model_width].reshape(row_count, KV_HEADS, repeats, HEAD_DIM),
        cosine[:, None, None, :],
        sine[:, None, None, :],
    ).astype(jnp.bfloat16)
    key_rows = rotate(
        projected[:, model_width : model_width + kv_width].reshape(row_count, KV_HEADS, HEAD_DIM),
        cosine[:, None, :],
        sine[:, None, :],
    ).astype(jnp.bfloat16)
    value_rows = projected[:, model_width + kv_width :].astype(jnp.bfloat16)
    key_local = key_rows.reshape(groups, local_len, kv_width)
    value_local = value_rows.reshape(groups, local_len, kv_width)
    all_keys, all_values = (
        lax.all_gather(key_local, "ctx", axis=1, tiled=True),
        lax.all_gather(value_local, "ctx", axis=1, tiled=True),
    )
    query_seq = query_rows.reshape(groups, local_len, KV_HEADS, repeats, HEAD_DIM)
    attended, logsum = lax.map(
        attend,
        (
            query_seq,
            all_keys.reshape(groups, SEQ_LEN, KV_HEADS, HEAD_DIM),
            all_values.reshape(groups, SEQ_LEN, KV_HEADS, HEAD_DIM),
            own_positions,
            positions,
        ),
    )
    attn_rows = attended.reshape(row_count, model_width).astype(jnp.bfloat16)
    middle = resid + jnp.dot(attn_rows, out_full, preferred_element_type=jnp.float32)
    gate_full, up_full, down_full = (
        lax.all_gather(w_gate, ("ctx", "shard"), axis=0, tiled=True),
        lax.all_gather(w_up, ("ctx", "shard"), axis=0, tiled=True),
        lax.all_gather(w_down, ("ctx", "shard"), axis=0, tiled=True),
    )
    second_inv = lax.rsqrt(jnp.mean(middle * middle, axis=-1, keepdims=True) + epsilon)
    normed_two = (middle * second_inv * gain_rows[1]).astype(jnp.bfloat16)
    gate_pre = jnp.dot(normed_two, gate_full, preferred_element_type=jnp.float32)
    up_pre = jnp.dot(normed_two, up_full, preferred_element_type=jnp.float32)
    sigmoid_gate = jax.nn.sigmoid(gate_pre)
    act_rows = (gate_pre * sigmoid_gate * up_pre).astype(jnp.bfloat16)
    final = middle + jnp.dot(act_rows, down_full, preferred_element_type=jnp.float32)
    block_out = final.astype(jnp.bfloat16).reshape(groups, local_len, model_width)
    qkv_back, out_back, gains_back = (
        lax.all_gather(w_qkv, ("ctx", "shard"), axis=0, tiled=True),
        lax.all_gather(w_out, ("ctx", "shard"), axis=0, tiled=True),
        lax.all_gather(norm_gains, ("ctx", "shard"), axis=1, tiled=True),
    )
    gate_back, up_back, down_back = (
        lax.all_gather(w_gate, ("ctx", "shard"), axis=0, tiled=True),
        lax.all_gather(w_up, ("ctx", "shard"), axis=0, tiled=True),
        lax.all_gather(w_down, ("ctx", "shard"), axis=0, tiled=True),
    )
    back_gains = gains_back.astype(jnp.float32)
    grad_top = cotangent.reshape(row_count, model_width)
    grad_down = jnp.einsum("tf,td->fd", act_rows, grad_top, preferred_element_type=jnp.float32)
    grad_act = jnp.einsum("td,fd->tf", grad_top, down_back, preferred_element_type=jnp.float32)
    grad_gate_rows = (
        grad_act * up_pre * sigmoid_gate * (1.0 + gate_pre * (1.0 - sigmoid_gate))
    ).astype(jnp.bfloat16)
    grad_up_rows = (grad_act * gate_pre * sigmoid_gate).astype(jnp.bfloat16)
    grad_gate = jnp.einsum(
        "td,tf->df", normed_two, grad_gate_rows, preferred_element_type=jnp.float32
    )
    grad_up = jnp.einsum("td,tf->df", normed_two, grad_up_rows, preferred_element_type=jnp.float32)
    grad_norm_two = jnp.einsum(
        "tf,df->td", grad_gate_rows, gate_back, preferred_element_type=jnp.float32
    ) + jnp.einsum("tf,df->td", grad_up_rows, up_back, preferred_element_type=jnp.float32)
    gain_two, grad_middle = norm_back(middle, second_inv, back_gains[1], grad_norm_two)
    grad_middle = grad_middle + grad_top.astype(jnp.float32)
    branch_rows = grad_middle.astype(jnp.bfloat16)
    grad_out = jnp.einsum("td,te->de", attn_rows, branch_rows, preferred_element_type=jnp.float32)
    grad_attended = jnp.einsum(
        "te,de->td", branch_rows, out_back, preferred_element_type=jnp.float32
    ).astype(jnp.bfloat16)
    back_keys, back_values = (
        lax.all_gather(key_local, "ctx", axis=1, tiled=True),
        lax.all_gather(value_local, "ctx", axis=1, tiled=True),
    )
    grad_query, grad_key, grad_value = lax.map(
        attend_back,
        (
            query_seq,
            back_keys.reshape(groups, SEQ_LEN, KV_HEADS, HEAD_DIM),
            back_values.reshape(groups, SEQ_LEN, KV_HEADS, HEAD_DIM),
            grad_attended.reshape(groups, local_len, KV_HEADS, repeats, HEAD_DIM),
            logsum,
            own_positions,
            positions,
        ),
    )
    own_key_grad, own_value_grad = (
        lax.psum_scatter(
            grad_key.reshape(groups, SEQ_LEN, kv_width).astype(jnp.bfloat16),
            "ctx",
            scatter_dimension=1,
            tiled=True,
        ).astype(jnp.float32),
        lax.psum_scatter(
            grad_value.reshape(groups, SEQ_LEN, kv_width).astype(jnp.bfloat16),
            "ctx",
            scatter_dimension=1,
            tiled=True,
        ).astype(jnp.float32),
    )
    query_back = rotate_back(
        grad_query.reshape(row_count, KV_HEADS, repeats, HEAD_DIM),
        cosine[:, None, None, :],
        sine[:, None, None, :],
    ).reshape(row_count, model_width)
    key_back = rotate_back(
        own_key_grad.reshape(row_count, KV_HEADS, HEAD_DIM), cosine[:, None, :], sine[:, None, :]
    ).reshape(row_count, kv_width)
    grad_proj = jnp.concatenate(
        [query_back, key_back, own_value_grad.reshape(row_count, kv_width)], axis=-1
    ).astype(jnp.bfloat16)
    grad_qkv = jnp.einsum("td,te->de", normed_one, grad_proj, preferred_element_type=jnp.float32)
    grad_bias = jnp.sum(grad_proj, axis=0, dtype=jnp.float32)
    grad_norm_one = jnp.einsum("te,de->td", grad_proj, qkv_back, preferred_element_type=jnp.float32)
    gain_one, grad_first = norm_back(resid, first_inv, back_gains[0], grad_norm_one)
    input_grad = (grad_middle + grad_first).reshape(groups, local_len, model_width)
    grad_gains = jnp.stack([gain_one, gain_two])
    qkv_cols = grad_qkv.shape[1]
    out_cols = grad_out.shape[1]
    gate_cols = grad_gate.shape[1]
    up_cols = grad_up.shape[1]
    down_cols = grad_down.shape[1]
    flat_qkv = grad_qkv.reshape(-1)
    flat_out = grad_out.reshape(-1)
    flat_gate = grad_gate.reshape(-1)
    flat_up = grad_up.reshape(-1)
    flat_down = grad_down.reshape(-1)
    attn_sums = (
        lax.psum_scatter(flat_qkv, ("ctx", "shard"), scatter_dimension=0, tiled=True),
        lax.psum_scatter(grad_bias, ("ctx", "shard"), scatter_dimension=0, tiled=True),
        lax.psum_scatter(flat_out, ("ctx", "shard"), scatter_dimension=0, tiled=True),
        lax.psum_scatter(grad_gains, ("ctx", "shard"), scatter_dimension=1, tiled=True),
    )
    mlp_sums = (
        lax.psum_scatter(flat_gate, ("ctx", "shard"), scatter_dimension=0, tiled=True),
        lax.psum_scatter(flat_up, ("ctx", "shard"), scatter_dimension=0, tiled=True),
        lax.psum_scatter(flat_down, ("ctx", "shard"), scatter_dimension=0, tiled=True),
    )
    totals = (
        lax.psum(attn_sums[0].astype(jnp.bfloat16), "replica").astype(jnp.float32),
        lax.psum(attn_sums[1].astype(jnp.bfloat16), "replica").astype(jnp.float32),
        lax.psum(attn_sums[2].astype(jnp.bfloat16), "replica").astype(jnp.float32),
        lax.psum(attn_sums[3].astype(jnp.bfloat16), "replica").astype(jnp.float32),
        lax.psum(mlp_sums[0].astype(jnp.bfloat16), "replica").astype(jnp.float32),
        lax.psum(mlp_sums[1].astype(jnp.bfloat16), "replica").astype(jnp.float32),
        lax.psum(mlp_sums[2].astype(jnp.bfloat16), "replica").astype(jnp.float32),
    )
    return (
        block_out,
        input_grad,
        totals[0].reshape(-1, qkv_cols),
        totals[1],
        totals[2].reshape(-1, out_cols),
        totals[3],
        totals[4].reshape(-1, gate_cols),
        totals[5].reshape(-1, up_cols),
        totals[6].reshape(-1, down_cols),
    )


def solution(mesh):
    placed = (
        P(("shard", "replica"), "ctx", None),
        P(("shard", "replica"), None),
        P(("ctx", "shard"), None),
        P(("ctx", "shard")),
        P(("ctx", "shard"), None),
        P(None, ("ctx", "shard")),
        P(("ctx", "shard"), None),
        P(("ctx", "shard"), None),
        P(("ctx", "shard"), None),
        P(("shard", "replica"), "ctx", None),
    )
    return jax.shard_map(
        local,
        mesh=mesh,
        in_specs=placed,
        out_specs=(
            P(("shard", "replica"), "ctx", None),
            P(("shard", "replica"), "ctx", None),
            P(("ctx", "shard"), None),
            P(("ctx", "shard")),
            P(("ctx", "shard"), None),
            P(None, ("ctx", "shard")),
            P(("ctx", "shard"), None),
            P(("ctx", "shard"), None),
            P(("ctx", "shard"), None),
        ),
        check_vma=False,
    )
```

profile of v0, /device:TPU:0, one launch (start us, length us, event | category | flops | bytes accessed | tf_op | source)
XLA Modules:
  0.0 3175.8 jit_solution(1888492155405357921)
XLA Ops:
  13.5 44.0 %all-reduce = bf16[1152]{0:T(1024)(128)(2,1)S(1)} all-reduce(bf16[1152]{0:T(1024)(128)(2,1)S(1)} %dynamic-update-slice), channel_id=1, replica_groups=mesh['ctx'=4,'shard'=4,'replica'=2] {'ctx','shard'}, use_global_device_ids=true, to_apply=%add | all-reduce | flops 1152 | bytes 4608
  57.4 35.6 %all-gather.2 = bf16[16,56,2]{1,2,0:T(2,128)(2,1)S(1)} all-gather(bf16[1,56,2]{1,2,0:T(2,128)(2,1)} %bitcast.157), channel_id=1, replica_groups=mesh['ctx'=4,'shard'=4,'replica'=2] {'ctx','shard'}, dimensions={0}, use_global_device_ids=true | all-gather | bytes 3808 | tf_op jit(solution)/shard_map/all_gather | solution.py:114
  102.3 7.7 all-gather
  111.2 9.4 all-gather.1
  122.2 7.4 fusion.59
  129.6 7.2 fusion.3
  136.8 6.8 fusion.10
  146.9 104.7 %all-gather.13.cloned.1.call-done = bf16[896,4864]{1,0:T(8,128)(2,1)} async-done(((bf16[56,4864]{1,0:T(8,128)(2,1)}), bf16[896,4864]{1,0:T(8,128)(2,1)}) %all-gather.13.cloned.1.call-update) | async-done | bytes 8716304 | tf_op jit(solution)/shard_map/all_gather | solution.py:155
  251.5 7.9 fusion.60
  259.4 108.9 %all-gather.15.cloned.1.call-done = bf16[896,4864]{1,0:T(8,128)(2,1)} async-done(((bf16[56,4864]{1,0:T(8,128)(2,1)}), bf16[896,4864]{1,0:T(8,128)(2,1)}) %all-gather.15.cloned.1.call-update) | async-done | bytes 8716304 | tf_op jit(solution)/shard_map/all_gather | solution.py:156
  368.3 7.9 fusion.61
  376.2 108.8 %all-gather.17.cloned.1.call-done = bf16[4864,896]{1,0:T(8,128)(2,1)} async-done(((bf16[304,896]{1,0:T(8,128)(2,1)}), bf16[4864,896]{1,0:T(8,128)(2,1)}) %all-gather.17.cloned.1.call-update) | async-done | bytes 8716304 | tf_op jit(solution)/shard_map/all_gather | solution.py:157
  485.0 11.4 multiply_convert_fusion
  496.4 8.1 fusion.62
  504.6 3.6 multiply_reduce_fusion
  511.9 8.3 fusion.17
  520.2 10.0 fusion
  532.6 9.0 fusion.63
  541.6 8.5 fusion.64
  550.1 7.0 fusion.2
  563.3 4.5 reshape.453
  567.7 17.8 reshape.456
  585.5 17.8 reshape.459
  603.3 10.4 fusion.33
  613.7 18.5 reshape.462
  632.3 5.4 broadcast_multiply_fusion
  642.1 18.9 reduce-scatter.6.cloned.1.call-done
  661.0 3.9 fusion.41
  665.2 4.7 reshape.450
  673.4 2438.7 %all-reduce.15 = (bf16[1032192]{0:T(1024)(128)(2,1)}, bf16[1152]{0:T(1024)(128)(2,1)S(1)}, bf16[802816]{0:T(1024)(128)(2,1)}, bf16[2,896]{1,0:T(2,128)(2,1)S(1)}...) all-reduce(f32[1032192]{0:T(1024)} %reshape.450, ...), channel_id=6, replica_groups=mesh['ctx'=4,'shard'=4,'replica'=2] {'ctx','shard'}, use_global_device_ids=true, to_apply=%region_10.11.clone | all-reduce | flops 14912384 | bytes 89474304
  3124.2 7.8 fusion.15
  3138.0 21.3 all-reduce.14.cloned.1.call-done
  (165 shorter events, 65.4 us)
Async XLA Ops:
  7.2 92.3 %all-gather.9.cloned.1.call-start = ((), (), s32[]{:S(2)}) async-start(), calls=%async_computation.2 | async-start | bytes 2193408 | tf_op jit(solution)/shard_map/all_gather | solution.py:111
  7.9 135.7 %all-gather.11.cloned.1.call-start = ((), (), s32[]{:S(2)}) async-start(), calls=%async_computation.3 | async-start | bytes 1705984 | tf_op jit(solution)/shard_map/all_gather | solution.py:113
  8.7 242.9 %all-gather.13.cloned.1.call-start = ((), (), s32[]{:S(2)}) async-start(), calls=%async_computation.4 | async-start | bytes 9261056 | tf_op jit(solution)/shard_map/all_gather | solution.py:155
  9.4 358.9 %all-gather.15.cloned.1.call-start = ((), (), s32[]{:S(2)}) async-start(), calls=%async_computation.5 | async-start | bytes 9261056 | tf_op jit(solution)/shard_map/all_gather | solution.py:156
  10.0 475.0 %all-gather.17.cloned.1.call-start = ((), (), s32[]{:S(2)}) async-start(), calls=%async_computation.6 | async-start | bytes 9261056 | tf_op jit(solution)/shard_map/all_gather | solution.py:157
  10.6 629.7 %reduce-scatter.4.cloned.1.call-start = ((), (), s32[]{:S(2)}) async-start(), calls=%async_computation.7 | async-start | bytes 327680 | tf_op jit(solution)/shard_map/reduce_scatter | solution.py:216
  94.8 16.4 copy-start.17
  122.2 7.4 copy-start.4
  129.6 7.2 copy-start.15
  136.8 6.9 copy-start.2
  136.8 9.9 copy-start.22
  143.6 115.8 %copy-start.10 = (bf16[2,64,7,256]{3,1,2,0:T(8,128)(2,1)}, bf16[2,64,7,256]{3,1,2,0:T(8,128)(2,1)S(1)}, u32[]{:S(2)}) copy-start(bf16[2,64,7,256]{3,1,2,0:T(8,128)(2,1)S(1)} %fusion.10) | copy-start | bytes 1376260
  146.7 357.8 %copy-start.26 = (f32[256]{0:T(256)}, f32[256]{0:T(256)S(1)}, u32[]{:S(2)}) copy-start(f32[256]{0:T(256)S(1)} %get-tuple-element.106) | copy-start | bytes 3076
  259.4 225.6 %copy-start.12 = (bf16[1,256,896]{2,1,0:T(8,128)(2,1)S(1)}, bf16[1,256,896]{2,1,0:T(8,128)(2,1)}, u32[]{:S(2)}) copy-start(bf16[1,256,896]{2,1,0:T(8,128)(2,1)} %param.19) | copy-start | bytes 1376260
  496.4 8.1 copy-start.8
  496.4 8.1 copy-start.6
  496.4 8.1 copy-start.1
  511.9 8.3 copy-start.16
  520.2 10.0 copy-start.11
  532.6 9.0 copy-start.7
  532.6 17.5 slice-start
  532.6 17.5 slice-start.1
  541.6 8.5 slice-start.2
  541.6 8.5 slice-start.3
  550.1 10.1 copy-start.5
  563.2 97.7 %reduce-scatter.6.cloned.1.call-start = ((), (), s32[]{:S(2)}) async-start(), calls=%async_computation.8 | async-start | bytes 327680 | tf_op jit(solution)/shard_map/reduce_scatter | solution.py:222
  585.5 17.8 copy-start.14
  613.7 18.5 copy-start.18
  637.7 23.3 copy-start.21
  637.7 23.3 copy-start.25
  638.5 2520.7 %all-reduce.14.cloned.1.call-start = ((), (), s32[]{:S(2)}) async-start(), calls=%async_computation.9 | async-start | bytes 3727360 | tf_op jit(solution)/shard_map/psum | solution.py:268
  3124.2 11.4 copy-start.27
  (10 other events, 37.1 us)
Sparse Core Ops, SparseCore 0:
  10.7 63.3 all-gather.8
  76.8 57.0 all-gather.10
  136.7 114.7 all-gather.12
  254.1 114.1 all-gather.14
  370.9 114.1 all-gather.16
  563.3 22.2 reduce-scatter.3
  638.7 22.2 reduce-scatter.5
  3123.0 36.2 all-reduce.13
where the time goes:
time: 3180 us
  blocking collectives  2540 us (80%)
  waiting for transfers between devices  366 us (12%)
  matrix products  132 us (4%)
  local copies, waits for them, and re-layouts  83.2 us (3%)
  other arithmetic  37.9 us (1%)
    unnamed x2, blocking collectives  2480 us
    all_gather x1, waiting for transfers between devices, local(): lax.all_gather(w_up, ('ctx', 'shard'), axis=0, tiled=True)  109 us
    all_gather x1, waiting for transfers between devices, local(): lax.all_gather(w_down, ('ctx', 'shard'), axis=0, tiled=True)  109 us
    all_gather x1, waiting for transfers between devices, local(): lax.all_gather(w_gate, ('ctx', 'shard'), axis=0, tiled=True)  105 us
  transfers between devices with their start and end apart: 8, of which 5 were waited for; matrix products, arithmetic and copies ran while one was open for 4% of the time, Pallas kernels for 0%

commit v1 on v0

v1 whole, which is shorter than its diff:
```python
import jax
import jax.numpy as jnp
from jax import lax
from jax.sharding import PartitionSpec as P

Q_HEADS = 14
KV_HEADS = 2
HEAD_DIM = 64
SEQ_LEN = 1024


epsilon = 1e-06
rope_base = 1000000.0
score_scale = 0.125
masked_value = -1e30


def rope_tables(positions):
    half_dim = HEAD_DIM // 2
    inverse = rope_base ** (-(jnp.arange(half_dim, dtype=jnp.float32) * 2.0) / HEAD_DIM)
    angles = positions.astype(jnp.float32)[..., None] * inverse
    angles = jnp.concatenate([angles, angles], axis=-1)
    return (jnp.cos(angles), jnp.sin(angles))


def rotate(values, cosine, sine):
    half_dim = values.shape[-1] // 2
    turned = jnp.concatenate([-values[..., half_dim:], values[..., :half_dim]], axis=-1)
    return values * cosine + turned * sine


def rotate_back(grads, cosine, sine):
    half_dim = grads.shape[-1] // 2
    moved = grads * sine
    turned = jnp.concatenate([moved[..., half_dim:], -moved[..., :half_dim]], axis=-1)
    return grads * cosine + turned


def norm_back(inputs, inverse, gain, upstream):
    scaled = upstream * gain
    gain_term = jnp.sum(upstream * inputs * inverse, axis=0)
    input_term = inverse * scaled - inputs * inverse**3 * jnp.mean(
        scaled * inputs, axis=-1, keepdims=True
    )
    return (gain_term, input_term)


def masked_scores(queries, key_rows, pos_query, pos_key):
    scores = (
        jnp.einsum("qhrd,khd->hrqk", queries, key_rows, preferred_element_type=jnp.float32)
        * score_scale
    )
    allowed = pos_query[:, None] >= pos_key[None, :]
    return jnp.where(allowed, scores, masked_value)


def attend(packed):
    queries, key_rows, value_rows, pos_query, pos_key = packed
    scores = masked_scores(queries, key_rows, pos_query, pos_key)
    top_score = jnp.max(scores, axis=-1, keepdims=True)
    weights = jnp.exp(scores - top_score)
    totals = jnp.sum(weights, axis=-1, keepdims=True)
    attn_probs = (weights / totals).astype(jnp.bfloat16)
    mixed_out = jnp.einsum(
        "hrqk,khd->qhrd", attn_probs, value_rows, preferred_element_type=jnp.float32
    )
    return (mixed_out, top_score + jnp.log(totals))


def attend_back(packed):
    queries, key_rows, value_rows, upstream, logsum, pos_query, pos_key = packed
    scores = masked_scores(queries, key_rows, pos_query, pos_key)
    attn_probs = jnp.exp(scores - logsum)
    dprob = jnp.einsum("qhrd,khd->hrqk", upstream, value_rows, preferred_element_type=jnp.float32)
    row_dot = jnp.sum(attn_probs * dprob, axis=-1, keepdims=True)
    dscore = (attn_probs * (dprob - row_dot)).astype(jnp.bfloat16)
    grad_query = (
        jnp.einsum("hrqk,khd->qhrd", dscore, key_rows, preferred_element_type=jnp.float32)
        * score_scale
    )
    grad_key = (
        jnp.einsum("hrqk,qhrd->khd", dscore, queries, preferred_element_type=jnp.float32)
        * score_scale
    )
    grad_value = jnp.einsum(
        "hrqk,qhrd->khd",
        attn_probs.astype(jnp.bfloat16),
        upstream,
        preferred_element_type=jnp.float32,
    )
    return (grad_query, grad_key, grad_value)


def swap(values):
    return lax.ppermute(values, "replica", [(0, 1), (1, 0)])


def pair_sum(parts):
    mine = lax.axis_index("replica")
    kept = lax.dynamic_index_in_dim(parts, mine, 0, keepdims=False)
    sent = lax.dynamic_index_in_dim(parts, 1 - mine, 0, keepdims=False)
    return kept.astype(jnp.float32) + swap(sent.astype(jnp.bfloat16)).astype(jnp.float32)


def pair_join(values):
    first = lax.axis_index("replica") == 0
    other = swap(values)
    return jnp.stack([jnp.where(first, values, other), jnp.where(first, other, values)])


def scatter_rows(partial):
    rows, width = partial.shape
    replica_count = lax.axis_size("replica")
    ctx_count = lax.axis_size("ctx")
    parts = partial.reshape(ctx_count, replica_count, -1, width).transpose(1, 0, 2, 3)
    parts = pair_sum(parts).astype(jnp.bfloat16)
    return lax.psum_scatter(parts, "ctx", scatter_dimension=0, tiled=False)


def owner_sum(grad):
    rows, width = grad.shape
    replica_count = lax.axis_size("replica")
    parts = grad.reshape(rows, replica_count, -1).transpose(1, 0, 2)
    parts = pair_sum(parts).astype(jnp.bfloat16)
    parts = lax.psum_scatter(parts, "ctx", scatter_dimension=0, tiled=True)
    parts = lax.psum_scatter(parts, "shard", scatter_dimension=0, tiled=True)
    both = pair_join(parts)
    return jnp.concatenate([both[0], both[1]], axis=1).astype(jnp.float32)


def local(tokens, block_order, w_qkv, qkv_bias, w_out, norm_gains, w_gate, w_up, w_down, cotangent):
    groups, local_len, model_width = tokens.shape
    kv_width = KV_HEADS * HEAD_DIM
    repeats = Q_HEADS // KV_HEADS
    ctx_count = lax.axis_size("ctx")
    shard_count = lax.axis_size("shard")
    replica_count = lax.axis_size("replica")
    ctx_index = lax.axis_index("ctx")
    shard_index = lax.axis_index("shard")
    replica_index = lax.axis_index("replica")
    owner_index = ctx_index * shard_count + shard_index
    block_len = local_len // 2
    row_count = groups * local_len
    own_rows, ff_width = w_gate.shape
    own_ff = w_down.shape[0]
    half_ff = own_ff // replica_count
    slice_ff = shard_count * half_ff
    qkv_width = w_qkv.shape[1]
    f32, bf16 = jnp.float32, jnp.bfloat16
    everyone = ("ctx", "shard", "replica")

    slots = jnp.arange(SEQ_LEN, dtype=jnp.int32)
    owners = (
        (slots // block_len)[:, None] == jnp.arange(2 * ctx_count, dtype=jnp.int32)[None, :]
    ).astype(jnp.int32)
    positions = (
        jnp.sum(block_order[:, None, :] * owners[None], axis=-1) * block_len + slots % block_len
    )
    own_positions = lax.dynamic_slice_in_dim(positions, ctx_index * local_len, local_len, 1)

    extra = jnp.concatenate([qkv_bias, norm_gains.reshape(-1)])
    extra = jnp.pad(extra, (0, qkv_width - extra.shape[0]))
    packed = lax.all_gather(
        jnp.concatenate([w_qkv, extra[None]], axis=0), ("ctx", "shard"), axis=0, tiled=False
    )
    qkv_full = packed[:, :own_rows].reshape(model_width, qkv_width)
    extras = packed[:, own_rows]
    bias_len = qkv_bias.shape[0]
    bias_full = extras[:, :bias_len].reshape(-1)
    gains_full = (
        extras[:, bias_len : bias_len + 2 * own_rows]
        .reshape(-1, 2, own_rows)
        .transpose(1, 0, 2)
        .reshape(2, model_width)
    )
    out_full = lax.all_gather(w_out, ("ctx", "shard"), axis=0, tiled=True)

    def unit_slice(weight):
        own = lax.dynamic_index_in_dim(
            weight.reshape(own_rows, ctx_count, shard_count, replica_count, half_ff),
            replica_index,
            3,
            keepdims=False,
        )
        return own.reshape(own_rows, ctx_count, slice_ff).transpose(1, 0, 2)

    gate_up = jnp.stack([unit_slice(w_gate), unit_slice(w_up)], axis=1)
    gate_up = lax.all_to_all(gate_up, "ctx", split_axis=0, concat_axis=0, tiled=True)
    gate_up = lax.all_gather(gate_up, "shard", axis=0, tiled=False)
    gate_up = gate_up.transpose(2, 1, 0, 3, 4).reshape(2, model_width, slice_ff)
    gate_part, up_part = gate_up[0], gate_up[1]
    down_part = lax.all_gather(
        lax.dynamic_slice_in_dim(w_down, replica_index * half_ff, half_ff, 0),
        "shard",
        axis=0,
        tiled=True,
    )
    grad_top = cotangent.reshape(row_count, model_width)
    top_all = lax.all_gather(grad_top, ("ctx", "replica"), axis=0, tiled=True)

    gain_rows = gains_full.astype(f32)
    resid = tokens.reshape(row_count, model_width).astype(f32)
    first_inv = lax.rsqrt(jnp.mean(resid * resid, axis=-1, keepdims=True) + epsilon)
    normed_one = (resid * first_inv * gain_rows[0]).astype(bf16)
    projected = jnp.dot(normed_one, qkv_full, preferred_element_type=f32) + bias_full.astype(f32)
    cosine, sine = rope_tables(own_positions.reshape(row_count))
    query_rows = rotate(
        projected[:, :model_width].reshape(row_count, KV_HEADS, repeats, HEAD_DIM),
        cosine[:, None, None, :],
        sine[:, None, None, :],
    ).astype(bf16)
    key_rows = rotate(
        projected[:, model_width : model_width + kv_width].reshape(row_count, KV_HEADS, HEAD_DIM),
        cosine[:, None, :],
        sine[:, None, :],
    ).astype(bf16)
    value_rows = projected[:, model_width + kv_width :].astype(bf16)
    kv_local = jnp.concatenate([key_rows.reshape(row_count, kv_width), value_rows], axis=-1)
    kv_all = lax.all_gather(
        kv_local.reshape(groups, local_len, 2 * kv_width), "ctx", axis=1, tiled=True
    )
    all_keys = kv_all[..., :kv_width].reshape(groups, SEQ_LEN, KV_HEADS, HEAD_DIM)
    all_values = kv_all[..., kv_width:].reshape(groups, SEQ_LEN, KV_HEADS, HEAD_DIM)
    query_seq = query_rows.reshape(groups, local_len, KV_HEADS, repeats, HEAD_DIM)
    attended, logsum = lax.map(
        attend, (query_seq, all_keys, all_values, own_positions, positions)
    )
    attn_rows = attended.reshape(row_count, model_width).astype(bf16)
    middle = resid + jnp.dot(attn_rows, out_full, preferred_element_type=f32)
    second_inv = lax.rsqrt(jnp.mean(middle * middle, axis=-1, keepdims=True) + epsilon)
    normed_two = (middle * second_inv * gain_rows[1]).astype(bf16)

    normed_all = lax.all_gather(normed_two, ("ctx", "replica"), axis=0, tiled=True)
    gate_pre = jnp.dot(normed_all, gate_part, preferred_element_type=f32)
    up_pre = jnp.dot(normed_all, up_part, preferred_element_type=f32)
    grad_act = jnp.einsum("td,fd->tf", top_all, down_part, preferred_element_type=f32)
    sigmoid_gate = jax.nn.sigmoid(gate_pre)
    act_rows = (gate_pre * sigmoid_gate * up_pre).astype(bf16)
    grad_gate_rows = (
        grad_act * up_pre * sigmoid_gate * (1.0 + gate_pre * (1.0 - sigmoid_gate))
    ).astype(bf16)
    grad_up_rows = (grad_act * gate_pre * sigmoid_gate).astype(bf16)
    norm_part = jnp.einsum(
        "tf,df->td", grad_gate_rows, gate_part, preferred_element_type=f32
    ) + jnp.einsum("tf,df->td", grad_up_rows, up_part, preferred_element_type=f32)
    grad_norm_two = scatter_rows(norm_part).astype(f32)
    out_part = jnp.dot(act_rows, down_part, preferred_element_type=f32)
    block_out = (
        (middle + scatter_rows(out_part).astype(f32))
        .astype(bf16)
        .reshape(groups, local_len, model_width)
    )

    grad_gate = jnp.einsum("td,tf->df", normed_all, grad_gate_rows, preferred_element_type=f32)
    grad_up = jnp.einsum("td,tf->df", normed_all, grad_up_rows, preferred_element_type=f32)
    grad_down = jnp.einsum("tf,td->fd", act_rows, top_all, preferred_element_type=f32)
    down_sum = lax.psum_scatter(
        grad_down.astype(bf16), "shard", scatter_dimension=0, tiled=True
    )
    grad_down = pair_join(down_sum).reshape(own_ff, model_width).astype(f32)
    pair = jnp.stack(
        [
            grad_gate.astype(bf16).reshape(ctx_count, shard_count, own_rows, slice_ff),
            grad_up.astype(bf16).reshape(ctx_count, shard_count, own_rows, slice_ff),
        ]
    ).transpose(2, 1, 0, 3, 4)
    pair = lax.psum_scatter(pair, "shard", scatter_dimension=0, tiled=False)
    pair = lax.all_to_all(pair, "ctx", split_axis=0, concat_axis=0, tiled=True)
    pair = pair_join(pair)
    pair = (
        pair.reshape(replica_count, ctx_count, 2, own_rows, shard_count, half_ff)
        .transpose(2, 3, 1, 4, 0, 5)
        .reshape(2, own_rows, ff_width)
        .astype(f32)
    )

    gain_two, grad_middle = norm_back(middle, second_inv, gain_rows[1], grad_norm_two)
    grad_middle = grad_middle + grad_top.astype(f32)
    branch_rows = grad_middle.astype(bf16)
    grad_out = jnp.einsum("td,te->de", attn_rows, branch_rows, preferred_element_type=f32)
    grad_attended = jnp.einsum(
        "te,de->td", branch_rows, out_full, preferred_element_type=f32
    ).astype(bf16)
    grad_query, grad_key, grad_value = lax.map(
        attend_back,
        (
            query_seq,
            all_keys,
            all_values,
            grad_attended.reshape(groups, local_len, KV_HEADS, repeats, HEAD_DIM),
            logsum,
            own_positions,
            positions,
        ),
    )
    kv_grad = jnp.concatenate(
        [
            grad_key.reshape(groups, SEQ_LEN, kv_width),
            grad_value.reshape(groups, SEQ_LEN, kv_width),
        ],
        axis=-1,
    ).astype(bf16)
    own_kv = lax.psum_scatter(kv_grad, "ctx", scatter_dimension=1, tiled=True).astype(f32)
    own_kv = own_kv.reshape(row_count, 2 * kv_width)
    query_back = rotate_back(
        grad_query.reshape(row_count, KV_HEADS, repeats, HEAD_DIM),
        cosine[:, None, None, :],
        sine[:, None, None, :],
    ).reshape(row_count, model_width)
    key_back = rotate_back(
        own_kv[:, :kv_width].reshape(row_count, KV_HEADS, HEAD_DIM),
        cosine[:, None, :],
        sine[:, None, :],
    ).reshape(row_count, kv_width)
    grad_proj = jnp.concatenate([query_back, key_back, own_kv[:, kv_width:]], axis=-1).astype(bf16)
    grad_qkv = jnp.einsum("td,te->de", normed_one, grad_proj, preferred_element_type=f32)
    grad_bias = jnp.sum(grad_proj, axis=0, dtype=f32)
    grad_norm_one = jnp.einsum("te,de->td", grad_proj, qkv_full, preferred_element_type=f32)
    gain_one, grad_first = norm_back(resid, first_inv, gain_rows[0], grad_norm_one)
    input_grad = (grad_middle + grad_first).reshape(groups, local_len, model_width)
    small = lax.psum(jnp.concatenate([grad_bias, gain_one, gain_two]), everyone)
    bias_sum = lax.dynamic_slice_in_dim(small[:qkv_width], owner_index * bias_len, bias_len, 0)
    gain_sum = lax.dynamic_slice_in_dim(
        small[qkv_width:].reshape(2, model_width), owner_index * own_rows, own_rows, 1
    )
    return (
        block_out,
        input_grad,
        owner_sum(grad_qkv),
        bias_sum,
        owner_sum(grad_out),
        gain_sum,
        pair[0],
        pair[1],
        grad_down,
    )


def solution(mesh):
    placed = (
        P(("shard", "replica"), "ctx", None),
        P(("shard", "replica"), None),
        P(("ctx", "shard"), None),
        P(("ctx", "shard")),
        P(("ctx", "shard"), None),
        P(None, ("ctx", "shard")),
        P(("ctx", "shard"), None),
        P(("ctx", "shard"), None),
        P(("ctx", "shard"), None),
        P(("shard", "replica"), "ctx", None),
    )
    return jax.shard_map(
        local,
        mesh=mesh,
        in_specs=placed,
        out_specs=(
            P(("shard", "replica"), "ctx", None),
            P(("shard", "replica"), "ctx", None),
            P(("ctx", "shard"), None),
            P(("ctx", "shard")),
            P(("ctx", "shard"), None),
            P(None, ("ctx", "shard")),
            P(("ctx", "shard"), None),
            P(("ctx", "shard"), None),
            P(("ctx", "shard"), None),
        ),
        check_vma=False,
    )
```

time: 3180 us -> 714 us (0.22)
  blocking collectives: 2540 us -> 66.5 us
  waiting for transfers between devices: 366 us -> 412 us
    unnamed x2 -> x0, blocking collectives: 2480 us -> none
    unnamed x8 -> x21, waiting for transfers between devices: 3.16 us -> 191 us
    all_gather x5 -> x6, waiting for transfers between devices: 322 us -> 189 us  [the longest x1 46.6 us: local(): gate_up = lax.all_gather(gate_up, 'shard', axis=0, tiled=False)]
    reshape x10 -> x8, local copies, waits for them, and re-layouts: 69 us -> 10.2 us  [the longest x2 8.52 us: unit_slice(): weight.reshape(own_rows, ctx_count, shard_count, replica_count, half_ff)]
    all_gather x3 -> x1, blocking collectives: 52.7 us -> 11.5 us  [local(): lax.all_gather(kv_local.reshape(groups, local_len, 2 * kv_width), 'ctx',...]
    psum x1, blocking collectives: 2.45 us -> 40.6 us  [local(): small = lax.psum(jnp.concatenate([grad_bias, gain_one, gain_two]), everyone)]
  transfers between devices with their start and end apart: 8 -> 23, of which waited for: 5 -> 18; matrix products, arithmetic and copies ran while one was open for 4% -> 19% of each run, Pallas kernels for 0% -> 0%
where the time goes in v1:
time: 714 us; the launch traced here: 709 us
  waiting for transfers between devices  412 us (58%)
  matrix products  102 us (14%)
  blocking collectives  66.5 us (9%)
  local copies, waits for them, and re-layouts  62.5 us (9%)
  other arithmetic  44.9 us (6%)
  between operations  15.9 us (2%)
    unnamed x21, waiting for transfers between devices  191 us
    all_gather x1, waiting for transfers between devices, local(): gate_up = lax.all_gather(gate_up, 'shard', axis=0, tiled=False)  46.6 us
    psum x1, blocking collectives, local(): small = lax.psum(jnp.concatenate([grad_bias, gain_one, gain_two]), everyone)  40.6 us
    all_gather x1, waiting for transfers between devices, local(): top_all = lax.all_gather(grad_top, ('ctx', 'replica'), axis=0, tiled=True)  35.8 us
    all_gather x1, waiting for transfers between devices, local(): lax.all_gather(jnp.concatenate([w_qkv, extra[None]], axis=0), ('ctx', 'sh...  32 us
    all_gather x1, waiting for transfers between devices, local(): lax.all_gather(normed_two, ('ctx', 'replica'), axis=0, tiled=True)  29.5 us
    all_gather x1, waiting for transfers between devices, local(): lax.all_gather(lax.dynamic_slice_in_dim(w_down, replica_index * half_ff,...  26.1 us
    all_gather x1, waiting for transfers between devices, local(): out_full = lax.all_gather(w_out, ('ctx', 'shard'), axis=0, tiled=True)  18.7 us
  transfers between devices with their start and end apart: 23, of which 18 were waited for; matrix products, arithmetic and copies ran while one was open for 19% of the time, Pallas kernels for 0%

profile of v1, /device:TPU:0, one launch (start us, length us, event | category | flops | bytes accessed | tf_op | source)
XLA Modules:
  0.0 709.4 jit_solution(6169923505261368428)
XLA Ops:
  19.7 6.2 dynamic-slice_reduce_fusion
  27.0 14.3 %all_to_all.10 = bf16[4,2,56,608]{3,2,1,0:T(8,128)(2,1)} all-to-all(bf16[4,2,56,608]{3,2,1,0:T(8,128)(2,1)S(1)} %copy.158), channel_id=1, replica_groups=mesh['ctx'=4,'shard'=4,'replica'=2] {'ctx'}, dimensions={0} | all-to-all | bytes 1089536 | tf_op jit(solution)/shard_map/all_to_all | solution.py:188
  44.4 32.0 %all-gather.22.cloned.1.call-done = bf16[16,57,1152]{2,1,0:T(8,128)(2,1)} async-done(((bf16[1,57,1152]{2,1,0:T(8,128)(2,1)}), bf16[16,57,1152]{2,1,0:T(8,128)(2,1)}) %all-gather.22.cloned.1.call-update) | async-done | bytes 2101264 | tf_op jit(solution)/shard_map/all_gather | solution.py:163
  83.1 11.5 %all-gather.1 = bf16[1024,256]{1,0:T(8,128)(2,1)S(1)} all-gather(bf16[256,256]{1,0:T(8,128)(2,1)S(1)} %pad_maximum_fusion.4), channel_id=3, replica_groups=mesh['ctx'=4,'shard'=4,'replica'=2] {'ctx'}, dimensions={0}, use_global_device_ids=true | all-gather | bytes 655360 | tf_op jit(solution)/shard_map/all_gather | solution.py:219
  96.0 7.4 %fusion.91 = (f32[2,7,256]{2,1,0:T(8,128)S(1)}, f32[2,7,256,1024]{2,3,1,0:T(8,128)}) fusion(bf16[1024,2,64,1]{0,2,3,1:T(8,128)(2,1)S(1)} %bitcast.267, bf16[256,2,7,64]{0,3,2,1:T(8,128)(2,1)S(1)} %fusion.59, pred[256,1024]{0,1:T(8,128)(4,1)S(1)} %broadcast_compare_fusion), kind=kOutput, calls=%fused_computation.189 | convolution fusion | flops 480768512 | bytes 15677440 | tf_op jit(solution)/shard_map/while/body/eval_jaxpr/qhrd,khd->hrqk/dot_general | solution.py:50
  103.4 7.2 %fusion.3 = f32[2,7,256]{2,1,0:T(8,128)S(1)} fusion(f32[2,7,256,1024]{2,3,1,0:T(8,128)} %get-tuple-element.144, f32[2,7,256]{2,1,0:T(8,128)S(1)} %get-tuple-element.143), kind=kLoop, calls=%fused_computation.9 | loop fusion | flops 7336448 | bytes 14708736 | tf_op jit(solution)/shard_map/while/body/eval_jaxpr/reduce_sum | solution.py:62
  110.6 6.6 fusion.27
  117.3 18.7 %all-gather.12.cloned.1.call-done = bf16[896,896]{1,0:T(8,128)(2,1)} async-done(((bf16[56,896]{1,0:T(8,128)(2,1)}), bf16[896,896]{1,0:T(8,128)(2,1)}) %all-gather.12.cloned.1.call-update) | async-done | bytes 1605648 | tf_op jit(solution)/shard_map/all_gather | solution.py:176
  139.2 46.6 %all-gather.18.cloned.1.call-done = bf16[16,2,56,608]{3,2,1,0:T(8,128)(2,1)} async-done(((bf16[4,2,56,608]{3,2,1,0:T(8,128)(2,1)}), bf16[16,2,56,608]{3,2,1,0:T(8,128)(2,1)}) %all-gather.18.cloned.1.call-update) | async-done | bytes 2179088 | tf_op jit(solution)/shard_map/all_gather | solution.py:189
  189.2 26.1 %all-gather.16.cloned.1.call-done = bf16[608,896]{1,0:T(8,128)(2,1)} async-done(((bf16[152,896]{1,0:T(8,128)(2,1)}), bf16[608,896]{1,0:T(8,128)(2,1)}) %all-gather.16.cloned.1.call-update) | async-done | bytes 1089552 | tf_op jit(solution)/shard_map/all_gather | solution.py:192
  215.3 35.8 %all-gather.20.cloned.1.call-done = bf16[1,2048,896]{2,1,0:T(8,128)(2,1)} async-done(((bf16[1,256,896]{2,1,0:T(8,128)(2,1)}), bf16[1,2048,896]{2,1,0:T(8,128)(2,1)}) %all-gather.20.cloned.1.call-update) | async-done | bytes 3670032 | tf_op jit(solution)/shard_map/all_gather | solution.py:199
  251.1 7.4 %fusion.17 = f32[608,2048]{1,0:T(8,128)} fusion(bf16[608,896]{1,0:T(8,128)(2,1)} %all-gather.16.cloned.1.call-done, bf16[1,2048,896]{2,1,0:T(8,128)(2,1)} %all-gather.20.cloned.1.call-done), kind=kOutput, calls=%fused_computation.27 | convolution fusion | flops 2231369728 | bytes 9740288 | tf_op jit(solution)/shard_map/td,fd->tf/dot_general | solution.py:236
  258.4 29.5 %all-gather.14.cloned.1.call-done = bf16[2048,896]{1,0:T(8,128)(2,1)} async-done(((bf16[256,896]{1,0:T(8,128)(2,1)}), bf16[2048,896]{1,0:T(8,128)(2,1)}) %all-gather.14.cloned.1.call-update) | async-done | bytes 3670032 | tf_op jit(solution)/shard_map/all_gather | solution.py:233
  287.9 7.5 %fusion.92 = f32[2048,608]{0,1:T(8,128)} fusion(bf16[2048,896]{1,0:T(8,128)(2,1)} %all-gather.14.cloned.1.call-done, bf16[896,608]{1,0:T(8,128)(2,1)} %bitcast.259), kind=kOutput, calls=%fused_computation.190 | convolution fusion | flops 2231369728 | bytes 9740288 | tf_op jit(solution)/shard_map/dot_general | solution.py:235
  295.4 8.4 %fusion.13 = (bf16[2048,608]{0,1:T(8,128)(2,1)S(1)}, bf16[2048,608]{0,1:T(8,128)(2,1)S(1)}, bf16[2048,608]{0,1:T(8,128)(2,1)}) fusion(f32[608,2048]{1,0:T(8,128)S(1)} %copy-done.29, f32[2048,608]{0,1:T(8,128)} %fusion.92, bf16[2048,896]{1,0:T(8,128)(2,1)S(1)} %copy-done.26, bf16[896,608]{1,0:T(8,128)(2,1)S(1)} %bitcast.278), kind=kOutput, calls=%fused_computation.20 | convolution fusion | flops 2251292672 | bytes 22192128 | tf_op jit(solution)/shard_map/dot_general | solution.py:234
  316.8 5.4 fusion.93
  328.0 21.7 %reduce-scatter.32.cloned.1.call-done = bf16[1,256,896]{2,1,0:T(8,128)(2,1)} async-done(((bf16[4,256,896]{2,1,0:T(8,128)(2,1)}), bf16[1,256,896]{2,1,0:T(8,128)(2,1)}) %reduce-scatter.32.cloned.1.call-update) | async-done | bytes 458768
  351.1 34.7 %reduce-scatter.30.cloned.1.call-done = bf16[1,256,896]{2,1,0:T(8,128)(2,1)} async-done(((bf16[4,256,896]{2,1,0:T(8,128)(2,1)}), bf16[1,256,896]{2,1,0:T(8,128)(2,1)}) %reduce-scatter.30.cloned.1.call-update) | async-done | bytes 458768
  390.6 8.3 %fusion.33 = bf16[2,64,1024]{2,1,0:T(8,128)(2,1)} fusion(bf16[256,2,7,64]{0,3,2,1:T(8,128)(2,1)S(1)} %bitcast.263, f32[2,7,256,1024]{2,3,1,0:T(8,128)} %get-tuple-element.144, f32[2,7,256]{2,1,0:T(8,128)S(1)} %log_add_fusion), kind=kOutput, calls=%fused_computation.57 | convolution fusion | flops 477233152 | bytes 15415296 | tf_op jit(solution)/shard_map/while/body/eval_jaxpr/hrqk,qhrd->khd/dot_general | solution.py:85
  398.9 9.7 %fusion = (f32[2,7,256]{2,1,0:T(8,128)S(1)}, f32[2,1024,256,7]{2,1,3,0:T(8,128)}) fusion(f32[2,7,256,1024]{2,3,1,0:T(8,128)} %get-tuple-element.144, f32[2,7,256]{2,1,0:T(8,128)S(1)} %log_add_fusion, bf16[1024,2,64,1]{0,2,3,1:T(8,128)(2,1)S(1)} %bitcast.283, bf16[256,2,7,64]{0,3,2,1:T(8,128)(2,1)S(1)} %bitcast.264), kind=kOutput, calls=%fused_computation.2 | convolution fusion | flops 480768512 | bytes 30109696 | tf_op jit(solution)/shard_map/while/body/eval_jaxpr/qhrd,khd->hrqk/dot_general | solution.py:74
  411.4 10.4 %fusion.2 = bf16[2,7,256,1024]{2,3,1,0:T(8,128)(2,1)S(1)} fusion(f32[2,1024,256,7]{2,1,3,0:T(8,128)} %get-tuple-element.148, f32[2,7,256,1024]{2,3,1,0:T(8,128)} %get-tuple-element.144, f32[2,7,256]{2,1,0:T(8,128)S(1)} %get-tuple-element.147, f32[2,7,256]{2,1,0:T(8,128)S(1)} %log_add_fusion), kind=kLoop, calls=%fused_computation.4 | loop fusion | flops 14680064 | bytes 36728832 | tf_op jit(solution)/shard_map/while/body/eval_jaxpr/convert_element_type | solution.py:76
  425.8 4.5 broadcast_multiply_fusion
  435.1 15.4 %reduce-scatter.22.cloned.1.call-done = bf16[1,256,256]{1,2,0:T(8,128)(2,1)} async-done(((bf16[1,1024,256]{1,2,0:T(8,128)(2,1)}), bf16[1,256,256]{1,2,0:T(8,128)(2,1)}) %reduce-scatter.22.cloned.1.call-update) | async-done | bytes 131088 | tf_op jit(solution)/shard_map/reduce_scatter | solution.py:303
  458.8 6.7 fusion.24
  465.6 6.6 convolution_convert_fusion
  472.1 8.9 %reduce-scatter.26.cloned.1.call-done = bf16[224,448]{1,0:T(8,128)(2,1)} async-done(((bf16[896,448]{1,0:T(8,128)(2,1)}), bf16[224,448]{1,0:T(8,128)(2,1)}) %reduce-scatter.26.cloned.1.call-update) | async-done | bytes 200720
  481.1 6.5 convolution_convert_fusion.1
  495.0 17.6 %reduce-scatter.24.cloned.1.call-done = bf16[224,576]{1,0:T(8,128)(2,1)} async-done(((bf16[896,576]{1,0:T(8,128)(2,1)}), bf16[224,576]{1,0:T(8,128)(2,1)}) %reduce-scatter.24.cloned.1.call-update) | async-done | bytes 258064
  514.5 28.6 %reduce-scatter.34.cloned.1.call-done = bf16[152,896]{1,0:T(8,128)(2,1)} async-done(((bf16[608,896]{1,0:T(8,128)(2,1)}), bf16[152,896]{1,0:T(8,128)(2,1)}) %reduce-scatter.34.cloned.1.call-update) | async-done | bytes 272400
  548.2 40.6 %psum.7 = f32[2944]{0:T(1024)S(1)} all-reduce(f32[2944]{0:T(1024)S(1)} %pad_maximum_fusion.7), channel_id=1, replica_groups=mesh['ctx'=4,'shard'=4,'replica'=2] {'ctx','shard','replica'}, use_global_device_ids=true, to_apply=%region_16.17 | all-reduce | flops 2944 | bytes 23552 | tf_op jit(solution)/shard_map/psum | solution.py:321
  591.1 78.0 %all-reduce.9.cloned.1.call-done = (bf16[224,576]{0,1:T(8,128)(2,1)}, bf16[4,4,2,56,608]{4,3,0,1,2:T(8,128)(2,1)}) async-done(((bf16[224,576]{0,1:T(8,128)(2,1)}, bf16[4,4,2,56,608]{4,3,0,1,2:T(8,128)(2,1)}), (bf16[224,576]{0,1:T(8,128)(2,1)}, bf16[4,4,2,56,608]{4,3,0,1,2:T(8,128)(2,1)})) %all-reduce.9.cloned.1.call-update) | async-done | bytes 2437136
  677.1 6.9 all-to-all-done.1
  (231 shorter events, 117.9 us)
Async XLA Ops:
  7.2 34.3 %copy-start = (bf16[304,896]{1,0:T(8,128)(2,1)S(1)}, bf16[304,896]{1,0:T(8,128)(2,1)}, u32[]{:S(2)}) copy-start(bf16[304,896]{1,0:T(8,128)(2,1)} %param.18) | copy-start | bytes 1634308
  7.2 69.2 %all-gather.22.cloned.1.call-start = ((), (), s32[]{:S(2)}) async-start(), calls=%async_computation.15 | async-start | bytes 2506752 | tf_op jit(solution)/shard_map/all_gather | solution.py:163
  10.4 125.6 %all-gather.12.cloned.1.call-start = ((), (), s32[]{:S(2)}) async-start(), calls=%async_computation.9 | async-start | bytes 1705984 | tf_op jit(solution)/shard_map/all_gather | solution.py:176
  11.1 174.7 %all-gather.18.cloned.1.call-start = ((), (), s32[]{:S(2)}) async-start(), calls=%async_computation.13 | async-start | bytes 2867200 | tf_op jit(solution)/shard_map/all_gather | solution.py:189
  26.8 16.0 %copy-start.5 = (bf16[1,256,896]{2,1,0:T(8,128)(2,1)S(1)}, bf16[1,256,896]{2,1,0:T(8,128)(2,1)}, u32[]{:S(2)}) copy-start(bf16[1,256,896]{2,1,0:T(8,128)(2,1)} %param.10) | copy-start | bytes 1376260
  27.0 16.1 %copy-start.25 = (s32[1,8]{1,0:T(1,128)S(1)}, s32[1,8]{1,0:T(1,128)}, u32[]{:S(2)}) copy-start(s32[1,8]{1,0:T(1,128)} %param.11) | copy-start | bytes 100
  41.4 173.9 %all-gather.16.cloned.1.call-start = ((), (), s32[]{:S(2)}) async-start(), calls=%async_computation.11 | async-start | bytes 1361920 | tf_op jit(solution)/shard_map/all_gather | solution.py:192
  42.2 208.9 %all-gather.20.cloned.1.call-start = ((), (), s32[]{:S(2)}) async-start(), calls=%async_computation.14 | async-start | bytes 4128768 | tf_op jit(solution)/shard_map/all_gather | solution.py:199
  42.8 245.1 %all-gather.14.cloned.1.call-start = ((), (), s32[]{:S(2)}) async-start(), calls=%async_computation.10 | async-start | bytes 4128768 | tf_op jit(solution)/shard_map/all_gather | solution.py:233
  117.2 21.9 %copy-start.16 = (bf16[2,64,7,256]{3,1,2,0:T(8,128)(2,1)}, bf16[2,64,7,256]{3,1,2,0:T(8,128)(2,1)S(1)}, u32[]{:S(2)}) copy-start(bf16[2,64,7,256]{3,1,2,0:T(8,128)(2,1)S(1)} %fusion.27) | copy-start | bytes 1376260
  139.2 210.6 %reduce-scatter.32.cloned.1.call-start = ((), (), s32[]{:S(2)}) async-start(), calls=%async_computation.20 | async-start | bytes 2293760
  311.0 3.9 collective-permute-start.1
  316.6 69.2 %reduce-scatter.30.cloned.1.call-start = ((), (), s32[]{:S(2)}) async-start(), calls=%async_computation.19 | async-start | bytes 2293760
  322.4 3.9 collective-permute-start
  327.9 57.9 %copy-start.14 = (bf16[1,256,896]{2,1,0:T(8,128)(2,1)S(1)}, bf16[1,256,896]{2,1,0:T(8,128)(2,1)}, u32[]{:S(2)}) copy-start(bf16[1,256,896]{2,1,0:T(8,128)(2,1)} %param.19) | copy-start | bytes 1376260
  328.0 122.5 %reduce-scatter.22.cloned.1.call-start = ((), (), s32[]{:S(2)}) async-start(), calls=%async_computation.12 | async-start | bytes 655360 | tf_op jit(solution)/shard_map/reduce_scatter | solution.py:303
  398.9 9.7 %copy-start.15 = (bf16[896,256]{0,1:T(8,128)(2,1)S(1)}, bf16[896,256]{0,1:T(8,128)(2,1)}, u32[]{:S(2)}) copy-start(bf16[896,256]{0,1:T(8,128)(2,1)} %get-tuple-element.101) | copy-start | bytes 1376260
  398.9 9.9 %copy-start.17 = (bf16[2,64,7,256]{3,1,2,0:T(8,128)(2,1)S(1)}, bf16[2,64,7,256]{3,1,2,0:T(8,128)(2,1)}, u32[]{:S(2)}) copy-start(bf16[2,64,7,256]{3,1,2,0:T(8,128)(2,1)} %copy-done.16) | copy-start | bytes 1376260
  410.6 20.0 %collective-permute-start.4 = (bf16[896,448]{0,1:T(8,128)(2,1)}, bf16[896,448]{0,1:T(8,128)(2,1)}, u32[]{:S(2)}, u32[]{:S(2)}) collective-permute-start(bf16[896,448]{0,1:T(8,128)(2,1)} %fusion.62), channel_id=1, source_target_pairs={{0,1},{1,0},{2,3},{3,2},{4,5},{5,4},{6,7},{7,6},{8,9},{9,8},{10,11... | collective-permute-start | bytes 2408456 | tf_op jit(solution)/shard_map/ppermute | solution.py:95
  425.6 55.5 %reduce-scatter.26.cloned.1.call-start = ((), (), s32[]{:S(2)}) async-start(), calls=%async_computation.17 | async-start | bytes 1146880
  435.1 77.5 %reduce-scatter.24.cloned.1.call-start = ((), (), s32[]{:S(2)}) async-start(), calls=%async_computation.16 | async-start | bytes 1433600
  454.4 2.7 collective-permute-start.2
  458.8 84.3 %reduce-scatter.34.cloned.1.call-start = ((), (), s32[]{:S(2)}) async-start(), calls=%async_computation.21 | async-start | bytes 1361920
  465.5 124.6 %reduce-scatter.28.cloned.1.call-start = ((), (), s32[]{:S(2)}) async-start(), calls=%async_computation.18 | async-start | bytes 286720
  481.1 188.1 %all-reduce.9.cloned.1.call-start = ((), (), s32[]{:S(2)}) async-start(), calls=%async_computation.22 | async-start | bytes 5177344
  495.0 48.0 %copy-start.27 = (u32[32]{0:T(128)S(1)}, u32[32]{0:T(128)}, u32[]{:S(2)}) copy-start(u32[32]{0:T(128)} %constant.192) | copy-start | bytes 388
  514.5 32.6 %copy-start.11 = (bf16[256,1152]{0,1:T(8,128)(2,1)S(1)}, bf16[256,1152]{0,1:T(8,128)(2,1)}, u32[]{:S(2)}) copy-start(bf16[256,1152]{0,1:T(8,128)(2,1)} %copy-done.10) | copy-start | bytes 1769476
  543.0 1.8 collective-permute-start.7
  591.0 85.6 %collective-permute-start.5 = (bf16[56,448]{0,1:T(8,128)(2,1)S(1)}, bf16[56,448]{0,1:T(8,128)(2,1)S(1)}, u32[]{:S(2)}, u32[]{:S(2)}) collective-permute-start(bf16[56,448]{0,1:T(8,128)(2,1)S(1)} %copy.192), channel_id=1, source_target_pairs={{0,1},{1,0},{2,3},{3,2},{4,5},{5,4},{6,7},{7,6},{8,9},{9,8},{10,11... | collective-permute-start | bytes 150536 | tf_op jit(solution)/shard_map/ppermute | solution.py:95
  671.8 12.2 %all-to-all-start.1 = ((bf16[4,2,56,608]{3,2,1,0:T(8,128)(2,1)}), bf16[4,2,56,608]{3,2,1,0:T(8,128)(2,1)S(1)}, u32[]{:S(2)}, u32[]{:S(2)}) async-start(bf16[4,2,56,608]{3,2,1,0:T(8,128)(2,1)} %copy_bitcast_fusion.1), calls=%async_computation.2 | async-start | bytes 1146880 | tf_op jit(solution)/shard_map/all_to_all | solution.py:268
  677.0 7.8 %collective-permute-start.3 = (bf16[56,576]{0,1:T(8,128)(2,1)S(1)}, bf16[56,576]{0,1:T(8,128)(2,1)S(1)}, u32[]{:S(2)}, u32[]{:S(2)}) collective-permute-start(bf16[56,576]{0,1:T(8,128)(2,1)S(1)} %constant_dynamic-slice_fusion.4), channel_id=1, source_target_pairs={{0,1},{1,0},{2,3},{3,2},{4,5},{5,4},{6,7},{7,6},{8,9},{9,8},{10,11... | collective-permute-start | bytes 193544 | tf_op jit(solution)/shard_map/ppermute | solution.py:95
  684.0 2.0 collective-permute-start.6
  (21 other events, 96.0 us)
Sparse Core Ops, SparseCore 0:
  11.4 64.9 all-gather.21
  79.0 56.8 all-gather.11
  137.5 48.2 all-gather.17
  187.8 27.4 all-gather.15
  217.0 33.9 all-gather.19
  253.4 34.5 all-gather.13
  316.7 32.9 reduce-scatter.31
  352.8 32.9 reduce-scatter.29
  425.7 24.7 reduce-scatter.21
  454.1 26.8 reduce-scatter.25
  484.2 28.3 reduce-scatter.23
  515.5 27.5 reduce-scatter.33
  545.4 18.8 reduce-scatter.27
  567.2 101.8 all-reduce.8
